TPU v7x, 32 devices: a whole 2x2x4 slice. The times are simulated.
32 devices in a mesh: gx: 8 (over z, core), gy: 4 (over y, x).
Axes of the slice: x: 2, y: 2, z: 4, core: 2. Of those that a mesh axis runs over, the one named last changes fastest.
Arguments:
- source: float32 [64, 64, 128], P('gx', 'gy'), may hold values from -6 to 6, as said below
- coupling_x: float32 [64, 64, 128], P('gx', 'gy'), may hold values from 128 to 512
- coupling_y: float32 [64, 64, 128], P('gx', 'gy'), may hold values from 128 to 512
- reaction: float32 [64, 64, 128], P('gx', 'gy'), may hold values from 0.03 to 0.12
Outputs:
- advanced: float32 [64, 64, 128], P('gx', 'gy')
Inputs may be any that keep to these rules, and one draw needn't show every extreme that they name: source terms of the sub-step.
All inputs are finite; a program needn't handle non-finite values.
Results may differ from a plain program's by a relative error of at most 0.002.
Values sent between devices are 32-bit elements; how exact they have to be, the bound alone decides.
A program may use at most 64 MiB of HBM per device.

v0:
```python
from functools import reduce

import jax
import jax.numpy as jnp
from jax import lax
from jax.sharding import PartitionSpec as P


def entering_2(x, axis, combine, identity, reverse):
    count, here = (lax.axis_size(axis), lax.axis_index(axis))
    everything = jax.tree.map(lambda part: lax.all_gather(part, axis), x)
    start = jax.tree.map(
        lambda part, zero: jnp.broadcast_to(jnp.asarray(zero, part.dtype), part.shape), x, identity
    )

    def turn(k, before):
        at = count - 1 - k if reverse else k
        reached = at > here if reverse else at < here
        new = combine(before, jax.tree.map(lambda part: part[at], everything))
        return jax.tree.map(lambda a, b: jnp.where(reached, a, b), new, before)

    return lax.fori_loop(0, count, turn, start)


def compose(left, right):
    entries = []
    for row_idx in range(3):
        for col_idx in range(3):
            entries.append(
                reduce(
                    lambda acc, term: acc + term,
                    [
                        left[3 * row_idx + mid_idx] * right[3 * mid_idx + col_idx]
                        for mid_idx in range(3)
                    ],
                )
            )
    largest = reduce(jnp.maximum, [jnp.abs(entry) for entry in entries])
    return tuple((entry / largest for entry in entries))


def chain_matrices(earlier, later):
    return compose(later, earlier)


def linked_transforms(earlier, later):
    return (later[0] + later[1] * earlier[0], later[1] * earlier[1])


def unit_matrix(sample):
    zero_field = jnp.zeros_like(sample)
    one_field = jnp.ones_like(sample)
    return (
        one_field,
        zero_field,
        zero_field,
        zero_field,
        one_field,
        zero_field,
        zero_field,
        zero_field,
        one_field,
    )


def cell_matrices(source, neighbor_coupling, reaction):
    zero_field = jnp.zeros_like(source)
    return (
        zero_field,
        zero_field,
        -neighbor_coupling,
        zero_field,
        neighbor_coupling,
        source,
        neighbor_coupling,
        zero_field,
        reaction + 2.0 * neighbor_coupling,
    )


def solve_lines(source, neighbor_coupling, reaction, solve_direction, enter_fn, leave_fn):
    prefix = lax.associative_scan(
        lambda earlier, later: compose(later, earlier),
        cell_matrices(source, neighbor_coupling, reaction),
        axis=solve_direction,
    )
    totals = tuple(
        (
            lax.index_in_dim(
                entry, entry.shape[solve_direction] - 1, solve_direction, keepdims=False
            )
            for entry in prefix
        )
    )
    entering = enter_fn(totals)
    state_x = jnp.expand_dims(entering[2], solve_direction)
    state_y = jnp.expand_dims(entering[5], solve_direction)
    state_z = jnp.expand_dims(entering[8], solve_direction)
    updated_streamwise = prefix[0] * state_x + prefix[1] * state_y + prefix[2] * state_z
    new_y = prefix[3] * state_x + prefix[4] * state_y + prefix[5] * state_z
    updated_normal = prefix[6] * state_x + prefix[7] * state_y + prefix[8] * state_z
    eliminate_factor = updated_streamwise / updated_normal
    offset_values = new_y / updated_normal

    def combine_transforms(later, current):
        return (current[0] + current[1] * later[0], current[1] * later[1])

    back_maps = lax.associative_scan(
        combine_transforms, (offset_values, -eliminate_factor), reverse=True, axis=solve_direction
    )
    first_maps = tuple(
        (lax.index_in_dim(entry, 0, solve_direction, keepdims=False) for entry in back_maps)
    )
    beyond = leave_fn(first_maps)
    return back_maps[0] + back_maps[1] * jnp.expand_dims(beyond, solve_direction)


def per_device(source, coupling_x, coupling_y, reaction):

    def x_enter(totals):
        return entering_2(totals, "gx", chain_matrices, unit_matrix(totals[0]), False)

    def x_leave(first_maps):
        return entering_2(
            first_maps,
            "gx",
            linked_transforms,
            (jnp.zeros_like(first_maps[0]), jnp.ones_like(first_maps[0])),
            True,
        )[0]

    halfway = solve_lines(source, coupling_x, reaction, 0, x_enter, x_leave)

    def y_enter(totals):
        return entering_2(totals, "gy", chain_matrices, unit_matrix(totals[0]), False)

    def y_leave(first_maps):
        return entering_2(
            first_maps,
            "gy",
            linked_transforms,
            (jnp.zeros_like(first_maps[0]), jnp.ones_like(first_maps[0])),
            True,
        )[0]

    advanced = solve_lines(halfway, coupling_y, reaction, 1, y_enter, y_leave)
    return advanced


def solution(mesh):
    placed = (P("gx", "gy", None), P("gx", "gy", None), P("gx", "gy", None), P("gx", "gy", None))
    return jax.shard_map(
        per_device, mesh=mesh, in_specs=placed, out_specs=P("gx", "gy", None), check_vma=False
    )
```

profile of v0, /device:TPU:0, one launch (start us, length us, event | category | flops | bytes accessed | tf_op | source)
XLA Modules:
  0.0 263.1 jit_solution(472724681547932231)
XLA Ops:
  0.0 1.0 copy_negate_fusion.1
  8.5 15.7 %all_gather.74 = f32[8,16,128]{2,1,0:T(8,128)S(1)} all-gather(f32[1,16,128]{2,1,0:T(8,128)S(1)} %bitcast.504), channel_id=1, replica_groups=mesh['gx'=8,'gy'=4] {'gx'}, dimensions={0}, use_global_device_ids=true | all-gather | bytes 73728 | tf_op jit(solution)/shard_map/all_gather | solution.py:11
  24.5 14.0 %all_gather.73 = f32[8,16,128]{2,1,0:T(8,128)S(1)} all-gather(f32[1,16,128]{2,1,0:T(8,128)S(1)} %bitcast.505), channel_id=1, replica_groups=mesh['gx'=8,'gy'=4] {'gx'}, dimensions={0}, use_global_device_ids=true | all-gather | bytes 73728 | tf_op jit(solution)/shard_map/all_gather | solution.py:11
  39.5 14.0 %all_gather.72 = f32[8,16,128]{2,1,0:T(8,128)S(1)} all-gather(f32[1,16,128]{2,1,0:T(8,128)S(1)} %bitcast.506), channel_id=1, replica_groups=mesh['gx'=8,'gy'=4] {'gx'}, dimensions={0}, use_global_device_ids=true | all-gather | bytes 73728 | tf_op jit(solution)/shard_map/all_gather | solution.py:11
  54.5 14.0 %all_gather.71 = f32[8,16,128]{2,1,0:T(8,128)S(1)} all-gather(f32[1,16,128]{2,1,0:T(8,128)S(1)} %bitcast.507), channel_id=1, replica_groups=mesh['gx'=8,'gy'=4] {'gx'}, dimensions={0}, use_global_device_ids=true | all-gather | bytes 73728 | tf_op jit(solution)/shard_map/all_gather | solution.py:11
  68.8 14.0 %all_gather.70 = f32[8,16,128]{2,1,0:T(8,128)S(1)} all-gather(f32[1,16,128]{2,1,0:T(8,128)S(1)} %bitcast.508), channel_id=1, replica_groups=mesh['gx'=8,'gy'=4] {'gx'}, dimensions={0}, use_global_device_ids=true | all-gather | bytes 73728 | tf_op jit(solution)/shard_map/all_gather | solution.py:11
  83.1 14.0 %all_gather.69 = f32[8,16,128]{2,1,0:T(8,128)S(1)} all-gather(f32[1,16,128]{2,1,0:T(8,128)S(1)} %bitcast.509), channel_id=1, replica_groups=mesh['gx'=8,'gy'=4] {'gx'}, dimensions={0}, use_global_device_ids=true | all-gather | bytes 73728 | tf_op jit(solution)/shard_map/all_gather | solution.py:11
  97.4 14.0 %all_gather.68 = f32[8,16,128]{2,1,0:T(8,128)S(1)} all-gather(f32[1,16,128]{2,1,0:T(8,128)S(1)} %bitcast.510), channel_id=1, replica_groups=mesh['gx'=8,'gy'=4] {'gx'}, dimensions={0}, use_global_device_ids=true | all-gather | bytes 73728 | tf_op jit(solution)/shard_map/all_gather | solution.py:11
  111.7 14.0 %all_gather.67 = f32[8,16,128]{2,1,0:T(8,128)S(1)} all-gather(f32[1,16,128]{2,1,0:T(8,128)S(1)} %bitcast.511), channel_id=1, replica_groups=mesh['gx'=8,'gy'=4] {'gx'}, dimensions={0}, use_global_device_ids=true | all-gather | bytes 73728 | tf_op jit(solution)/shard_map/all_gather | solution.py:11
  126.0 14.0 %all_gather.66 = f32[8,16,128]{2,1,0:T(8,128)S(1)} all-gather(f32[1,16,128]{2,1,0:T(8,128)S(1)} %bitcast.512), channel_id=1, replica_groups=mesh['gx'=8,'gy'=4] {'gx'}, dimensions={0}, use_global_device_ids=true | all-gather | bytes 73728 | tf_op jit(solution)/shard_map/all_gather | solution.py:11
  140.0 0.9 while.92
  143.1 14.0 %all_gather.76 = f32[8,16,128]{2,1,0:T(8,128)S(1)} all-gather(f32[1,16,128]{2,1,0:T(8,128)S(1)} %bitcast.513), channel_id=1, replica_groups=mesh['gx'=8,'gy'=4] {'gx'}, dimensions={0}, use_global_device_ids=true | all-gather | bytes 73728 | tf_op jit(solution)/shard_map/all_gather | solution.py:11
  157.4 14.1 %all_gather.75 = f32[8,16,128]{2,1,0:T(8,128)S(1)} all-gather(f32[1,16,128]{2,1,0:T(8,128)S(1)} %bitcast.514), channel_id=1, replica_groups=mesh['gx'=8,'gy'=4] {'gx'}, dimensions={0}, use_global_device_ids=true | all-gather | bytes 73728 | tf_op jit(solution)/shard_map/all_gather | solution.py:11
  174.6 8.2 %all-gather.8 = f32[32,1,128]{2,1,0:T(1,128)S(1)} all-gather(f32[8,1,128]{2,1,0:T(1,128)S(1)} %bitcast.532), channel_id=10, replica_groups=mesh['gx'=8,'gy'=4] {'gy'}, dimensions={0}, use_global_device_ids=true | all-gather | bytes 20480 | tf_op jit(solution)/shard_map/all_gather | solution.py:11
  182.9 8.1 %all-gather.7 = f32[32,1,128]{2,1,0:T(1,128)S(1)} all-gather(f32[8,1,128]{2,1,0:T(1,128)S(1)} %bitcast.533), channel_id=9, replica_groups=mesh['gx'=8,'gy'=4] {'gy'}, dimensions={0}, use_global_device_ids=true | all-gather | bytes 20480 | tf_op jit(solution)/shard_map/all_gather | solution.py:11
  191.2 7.2 %all-gather.6 = f32[32,1,128]{2,1,0:T(1,128)S(1)} all-gather(f32[8,1,128]{2,1,0:T(1,128)S(1)} %bitcast.534), channel_id=8, replica_groups=mesh['gx'=8,'gy'=4] {'gy'}, dimensions={0}, use_global_device_ids=true | all-gather | bytes 20480 | tf_op jit(solution)/shard_map/all_gather | solution.py:11
  198.6 8.1 %all-gather.5 = f32[32,1,128]{2,1,0:T(1,128)S(1)} all-gather(f32[8,1,128]{2,1,0:T(1,128)S(1)} %bitcast.535), channel_id=7, replica_groups=mesh['gx'=8,'gy'=4] {'gy'}, dimensions={0}, use_global_device_ids=true | all-gather | bytes 20480 | tf_op jit(solution)/shard_map/all_gather | solution.py:11
  206.9 7.2 %all-gather.4 = f32[32,1,128]{2,1,0:T(1,128)S(1)} all-gather(f32[8,1,128]{2,1,0:T(1,128)S(1)} %bitcast.536), channel_id=6, replica_groups=mesh['gx'=8,'gy'=4] {'gy'}, dimensions={0}, use_global_device_ids=true | all-gather | bytes 20480 | tf_op jit(solution)/shard_map/all_gather | solution.py:11
  214.2 8.2 %all-gather.3 = f32[32,1,128]{2,1,0:T(1,128)S(1)} all-gather(f32[8,1,128]{2,1,0:T(1,128)S(1)} %bitcast.537), channel_id=5, replica_groups=mesh['gx'=8,'gy'=4] {'gy'}, dimensions={0}, use_global_device_ids=true | all-gather | bytes 20480 | tf_op jit(solution)/shard_map/all_gather | solution.py:11
  222.6 7.2 %all-gather.2 = f32[32,1,128]{2,1,0:T(1,128)S(1)} all-gather(f32[8,1,128]{2,1,0:T(1,128)S(1)} %bitcast.538), channel_id=4, replica_groups=mesh['gx'=8,'gy'=4] {'gy'}, dimensions={0}, use_global_device_ids=true | all-gather | bytes 20480 | tf_op jit(solution)/shard_map/all_gather | solution.py:11
  229.9 8.1 %all-gather.1 = f32[32,1,128]{2,1,0:T(1,128)S(1)} all-gather(f32[8,1,128]{2,1,0:T(1,128)S(1)} %bitcast.539), channel_id=3, replica_groups=mesh['gx'=8,'gy'=4] {'gy'}, dimensions={0}, use_global_device_ids=true | all-gather | bytes 20480 | tf_op jit(solution)/shard_map/all_gather | solution.py:11
  238.2 7.2 %all-gather = f32[32,1,128]{2,1,0:T(1,128)S(1)} all-gather(f32[8,1,128]{2,1,0:T(1,128)S(1)} %bitcast.540), channel_id=2, replica_groups=mesh['gx'=8,'gy'=4] {'gy'}, dimensions={0}, use_global_device_ids=true | all-gather | bytes 20480 | tf_op jit(solution)/shard_map/all_gather | solution.py:11
  246.8 8.1 %all-gather.10 = f32[32,1,128]{2,1,0:T(1,128)S(1)} all-gather(f32[8,1,128]{2,1,0:T(1,128)S(1)} %bitcast.541), channel_id=12, replica_groups=mesh['gx'=8,'gy'=4] {'gy'}, dimensions={0}, use_global_device_ids=true | all-gather | bytes 20480 | tf_op jit(solution)/shard_map/all_gather | solution.py:11
  255.1 7.2 %all-gather.9 = f32[32,1,128]{2,1,0:T(1,128)S(1)} all-gather(f32[8,1,128]{2,1,0:T(1,128)S(1)} %bitcast.542), channel_id=11, replica_groups=mesh['gx'=8,'gy'=4] {'gy'}, dimensions={0}, use_global_device_ids=true | all-gather | bytes 20480 | tf_op jit(solution)/shard_map/all_gather | solution.py:11
  (450 shorter events, 19.6 us)
Async XLA Ops:
  1.0 0.8 copy-start
  1.1 0.9 copy-start.1
  38.6 0.7 slice-start
  53.6 0.7 slice-start.1
where the time goes:
time: 264 us; the launch traced here: 263 us
  blocking collectives  240 us (91%)
  local copies, waits for them, and re-layouts  14.5 us (5%)
  other arithmetic  5.25 us (2%)
    all_gather x22, blocking collectives, entering_2(): everything = jax.tree.map(lambda part: lax.all_gather(part, axis), x)  240 us
    pad x90, local copies, waits for them, and re-layouts, solve_lines(): lax.associative_scan(lambda earlier, later: compose(later, earlier), cell...  8.16 us

commit v1 on v0

v1 whole, which is shorter than its diff:
```python
import functools

import jax
import jax.numpy as jnp
from jax import lax
from jax.experimental import pallas as pl
from jax.experimental.pallas import tpu as pltpu
from jax.sharding import PartitionSpec as P

MESH = pl.DeviceIdType.MESH
LONG = 128


def sweep(prev, slope, s, g):
    here = prev + slope
    if g is None:
        return here, slope + s * here
    return here, (slope - g) + s * here


def join_coefs(maps, long):
    one = jnp.ones_like(maps[0][0])
    zero = jnp.zeros_like(one)
    if long:
        ratio, out = zero, []
        for a, b, c, d in maps:
            inv = 1.0 / (c * ratio + d)
            nxt = (a * ratio + b) * inv
            out.append((ratio, inv, nxt))
            ratio = nxt
        return out, 1.0 / (1.0 + ratio)
    hu, hd, out = zero, one, []
    for a, b, c, d in maps:
        out.append((hu, hd))
        hu, hd = a * hu + b * hd, c * hu + d * hd
    return out, 1.0 / (hu + hd)


def join(maps, offs, coefs, long):
    steps, last = coefs
    zero = jnp.zeros_like(last)
    if long:
        sigma, sig = zero, []
        for (a, b, c, d), (p, q), (_, _, nxt) in zip(maps, offs, steps):
            sig.append(sigma)
            sigma = (a * sigma + p) - nxt * (c * sigma + q)
        slope, states = -sigma * last, []
        for k in reversed(range(len(maps))):
            ratio, inv, _ = steps[k]
            slope = (slope - (maps[k][2] * sig[k] + offs[k][1])) * inv
            states.append((ratio * slope + sig[k], slope))
        return states[::-1]
    u, s, part = zero, zero, []
    for (a, b, c, d), (p, q) in zip(maps, offs):
        part.append((u, s))
        u, s = (a * u + b * s) + p, (c * u + d * s) + q
    t = -(u + s) * last
    return [(pu + t * hu, ps + t * hd) for (pu, ps), (hu, hd) in zip(part, steps)]


def kernel(nx, ny, lx, ly, owners, f_ref, kx_ref, ky_ref, r_ref, out_ref,
           seg_s, seg_r, ent_s, ent_r, yc, yo, sy_v, g_v,
           seg_ss, seg_rs, ent_ss, ent_rs, yc_ss, yc_rs, yo_ss, yo_rs):
    gx, gy = lax.axis_index("gx"), lax.axis_index("gy")
    every = nx // owners
    rows = ly // owners
    mine = gx // every

    barrier = pltpu.get_barrier_semaphore()
    for k in range(1, nx):
        pl.semaphore_signal(barrier, inc=1, device_id=(lax.rem(gx + k, nx), gy), device_id_type=MESH)
    for k in range(1, ny):
        pl.semaphore_signal(barrier, inc=1, device_id=(gx, lax.rem(gy + k, ny)), device_id_type=MESH)

    one = jnp.ones((ly, f_ref.shape[1]), jnp.float32)
    zero = jnp.zeros_like(one)
    h1, h2, h3 = (one, zero), (zero, one), (zero, zero)
    cells = []
    for i in range(lx):
        at = pl.ds(i * ly, ly)
        inv = 1.0 / kx_ref[at, :]
        s, g = r_ref[at, :] * inv, f_ref[at, :] * inv
        h1, h2, h3 = sweep(*h1, s, None), sweep(*h2, s, None), sweep(*h3, s, g)
        cells.append((h1[0], h2[0], h3[0]))
    for v, val in enumerate((h1[0], h2[0], h1[1], h2[1], h3[0], h3[1])):
        for o in range(owners):
            seg_s[o, v] = val[o * rows:(o + 1) * rows, :]

    pl.semaphore_wait(barrier, nx - 1 + ny - 1)

    def seg_copy(o):
        return pltpu.make_async_remote_copy(
            src_ref=seg_s.at[o], dst_ref=seg_r.at[gx],
            send_sem=seg_ss.at[o], recv_sem=seg_rs.at[gx],
            device_id=(o * every, gy), device_id_type=MESH)

    for k in range(1, owners):
        seg_copy(lax.rem(mine + k, owners)).start()
    if every > 1:
        @pl.when(lax.rem(gx, every) != 0)
        def _():
            seg_copy(mine).start()

    ivals = []
    for i in range(lx):
        at = pl.ds(i * ly, ly)
        inv = 1.0 / ky_ref[at, :]
        ivals.append(inv)
        sy_v[at, :] = r_ref[at, :] * inv
    one8 = jnp.ones((lx, f_ref.shape[1]), jnp.float32)
    zero8 = jnp.zeros_like(one8)
    y1, y2, ycells, sy = (one8, zero8), (zero8, one8), [], []
    for j in range(ly):
        s = sy_v[pl.ds(j, lx, stride=ly), :]
        sy.append(s)
        y1, y2 = sweep(*y1, s, None), sweep(*y2, s, None)
        ycells.append((y1[0], y2[0]))
    for v, val in enumerate((y1[0], y2[0], y1[1], y2[1])):
        yc[gy, v] = val

    def y_copy(buf, ss, rs, k):
        to = lax.rem(gy + k, ny)
        return pltpu.make_async_remote_copy(
            src_ref=buf.at[gy], dst_ref=buf.at[gy],
            send_sem=ss.at[to], recv_sem=rs.at[gy],
            device_id=(gx, to), device_id_type=MESH)

    def y_arrived(buf, ss, rs, k):
        frm = lax.rem(gy + k, ny)
        pltpu.make_async_remote_copy(
            src_ref=buf.at[frm], dst_ref=buf.at[frm],
            send_sem=ss.at[frm], recv_sem=rs.at[frm],
            device_id=(gx, frm), device_id_type=MESH).wait_recv()

    for k in range(1, ny):
        y_copy(yc, yc_ss, yc_rs, k).start()

    def ent_copy(to):
        return pltpu.make_async_remote_copy(
            src_ref=ent_s.at[to], dst_ref=ent_r.at[mine],
            send_sem=ent_ss.at[to], recv_sem=ent_rs.at[mine],
            device_id=(to, gy), device_id_type=MESH)

    def own():
        seg_r[gx] = seg_s[mine]
        for k in range(1, nx):
            frm = lax.rem(gx + k, nx)
            pltpu.make_async_remote_copy(
                src_ref=seg_s.at[0], dst_ref=seg_r.at[frm],
                send_sem=seg_ss.at[0], recv_sem=seg_rs.at[frm],
                device_id=(frm, gy), device_id_type=MESH).wait_recv()
        maps = [tuple(seg_r[d, v] for v in range(4)) for d in range(nx)]
        offs = [tuple(seg_r[d, v] for v in (4, 5)) for d in range(nx)]
        long = nx * lx > LONG
        for d, (u, s) in enumerate(join(maps, offs, join_coefs(maps, long), long)):
            ent_s[d, 0] = u
            ent_s[d, 1] = s
        for k in range(1, nx):
            ent_copy(lax.rem(gx + k, nx)).start()
        ent_r[mine] = ent_s[gx]

    if every > 1:
        pl.when(lax.rem(gx, every) == 0)(own)
    else:
        own()

    for k in range(1, ny):
        y_arrived(yc, yc_ss, yc_rs, k)
    ymaps = [tuple(yc[d, v] for v in range(4)) for d in range(ny)]
    ylong = ny * ly > LONG
    ycoefs = join_coefs(ymaps, ylong)

    def ent_arrived(o):
        pltpu.make_async_remote_copy(
            src_ref=ent_s.at[0], dst_ref=ent_r.at[o],
            send_sem=ent_ss.at[0], recv_sem=ent_rs.at[o],
            device_id=(o * every, gy), device_id_type=MESH).wait_recv()

    for k in range(1, owners):
        ent_arrived(lax.rem(mine + k, owners))
    if every > 1:
        @pl.when(lax.rem(gx, every) != 0)
        def _():
            ent_arrived(mine)

    u0 = jnp.concatenate([ent_r[o, 0] for o in range(owners)], axis=0)
    s0 = jnp.concatenate([ent_r[o, 1] for o in range(owners)], axis=0)
    for i in range(lx):
        ca, cb, cg = cells[i]
        g_v[pl.ds(i * ly, ly), :] = ((ca * u0 + cb * s0) + cg) * ivals[i]

    y3, ygs = (zero8, zero8), []
    for j in range(ly):
        y3 = sweep(*y3, sy[j], g_v[pl.ds(j, lx, stride=ly), :])
        ygs.append(y3[0])
    yo[gy, 0] = y3[0]
    yo[gy, 1] = y3[1]
    for k in range(1, ny):
        y_copy(yo, yo_ss, yo_rs, k).start()
    for k in range(1, ny):
        y_arrived(yo, yo_ss, yo_rs, k)
    yoffs = [(yo[d, 0], yo[d, 1]) for d in range(ny)]
    u, s = zero8, zero8
    for d, (du, ds) in enumerate(join(ymaps, yoffs, ycoefs, ylong)):
        here = gy == d
        u, s = jnp.where(here, du, u), jnp.where(here, ds, s)
    for j in range(ly):
        ca, cb = ycells[j]
        out_ref[pl.ds(j, lx, stride=ly), :] = (ca * u + cb * s) + ygs[j]

    for k in range(1, owners):
        seg_copy(lax.rem(mine + k, owners)).wait_send()
    if every > 1:
        @pl.when(lax.rem(gx, every) != 0)
        def _():
            seg_copy(mine).wait_send()

    def own_sent():
        for k in range(1, nx):
            ent_copy(lax.rem(gx + k, nx)).wait_send()

    if every > 1:
        pl.when(lax.rem(gx, every) == 0)(own_sent)
    else:
        own_sent()
    for k in range(1, ny):
        y_copy(yc, yc_ss, yc_rs, k).wait_send()
        y_copy(yo, yo_ss, yo_rs, k).wait_send()


def solution(mesh):
    nx, ny = mesh.shape["gx"], mesh.shape["gy"]

    def per_device(source, coupling_x, coupling_y, reaction):
        lx, ly, nz = source.shape
        owners = min(nx, ly // 2)
        rows = ly // owners
        f32 = jnp.float32
        dma = pltpu.SemaphoreType.DMA
        vmem = pl.BlockSpec(memory_space=pltpu.VMEM)
        flat = [a.reshape(lx * ly, nz) for a in (source, coupling_x, coupling_y, reaction)]
        out = pl.pallas_call(
            functools.partial(kernel, nx, ny, lx, ly, owners),
            out_shape=jax.ShapeDtypeStruct((lx * ly, nz), f32),
            in_specs=[vmem] * 4,
            out_specs=vmem,
            scratch_shapes=[
                pltpu.VMEM((owners, 6, rows, nz), f32),
                pltpu.VMEM((nx, 6, rows, nz), f32),
                pltpu.VMEM((nx, 2, rows, nz), f32),
                pltpu.VMEM((owners, 2, rows, nz), f32),
                pltpu.VMEM((ny, 4, lx, nz), f32),
                pltpu.VMEM((ny, 2, lx, nz), f32),
                pltpu.VMEM((lx * ly, nz), f32),
                pltpu.VMEM((lx * ly, nz), f32),
                dma((owners,)), dma((nx,)), dma((nx,)), dma((owners,)),
                dma((ny,)), dma((ny,)), dma((ny,)), dma((ny,)),
            ],
            compiler_params=pltpu.CompilerParams(
                collective_id=0, has_side_effects=True, vmem_limit_bytes=8 * 1024 * 1024),
        )(*flat)
        return out.reshape(lx, ly, nz)

    spec = P("gx", "gy", None)
    return jax.shard_map(per_device, mesh=mesh, in_specs=(spec,) * 4, out_specs=spec, check_vma=False)
```

time: 264 us -> 21.3 us (0.08)
  blocking collectives: 240 us -> 0 us
  Pallas kernels: 0 us -> 17 us
  local copies, waits for them, and re-layouts: 14.5 us -> 3.99 us
  other arithmetic: 5.25 us -> 0 us
    all_gather x22 -> x0, blocking collectives: 240 us -> none  [entering_2(): everything = jax.tree.map(lambda part: lax.all_gather(part, axis), x)]
    pallas_call x0 -> x1, Pallas kernels: none -> 17 us  [per_device(): pl.pallas_call(functools.partial(kernel, nx, ny, lx, ly, owners), out_sha...]
    pad x110 -> x0, local copies, waits for them, and re-layouts: 9.98 us -> none  [the longest x90 8.16 us: solve_lines(): lax.associative_scan(lambda earlier, later: compose(later, earlier), cell...]
    unnamed x5 -> x9, local copies, waits for them, and re-layouts: 0.81 us -> 3.99 us
    slice x92 -> x0, local copies, waits for them, and re-layouts: 2.94 us -> none  [the longest x66 2.31 us: solve_lines(): lax.associative_scan(lambda earlier, later: compose(later, earlier), cell...]
where the time goes in v1:
time: 21.3 us; the launch traced here: 21 us
  Pallas kernels  17 us (80%)
  local copies, waits for them, and re-layouts  3.99 us (19%)
    pallas_call x1, Pallas kernels, per_device(): pl.pallas_call(functools.partial(kernel, nx, ny, lx, ly, owners), out_sha...  17 us
    unnamed x9, local copies, waits for them, and re-layouts  3.99 us

profile of v1, /device:TPU:0, one launch (start us, length us, event | category | flops | bytes accessed | tf_op | source)
XLA Modules:
  0.0 21.0 jit_solution(13970812610247565916)
XLA Ops:
  0.0 0.0 copy-start
  0.0 0.8 %copy-done = f32[8,16,128]{2,1,0:T(8,128)S(1)} copy-done((f32[8,16,128]{2,1,0:T(8,128)S(1)}, f32[8,16,128]{2,1,0:T(8,128)}, u32[]{:S(2)}) %copy-start) | copy-done | bytes 65560
  0.8 0.0 copy-start.1
  0.8 0.8 %copy-done.1 = f32[8,16,128]{2,1,0:T(8,128)S(1)} copy-done((f32[8,16,128]{2,1,0:T(8,128)S(1)}, f32[8,16,128]{2,1,0:T(8,128)}, u32[]{:S(2)}) %copy-start.1) | copy-done | bytes 65560
  1.7 0.0 copy-start.2
  1.7 0.8 %copy-done.2 = f32[8,16,128]{2,1,0:T(8,128)S(1)} copy-done((f32[8,16,128]{2,1,0:T(8,128)S(1)}, f32[8,16,128]{2,1,0:T(8,128)}, u32[]{:S(2)}) %copy-start.2) | copy-done | bytes 65560
  2.5 0.0 copy-start.3
  2.5 0.8 %copy-done.3 = f32[8,16,128]{2,1,0:T(8,128)S(1)} copy-done((f32[8,16,128]{2,1,0:T(8,128)S(1)}, f32[8,16,128]{2,1,0:T(8,128)}, u32[]{:S(2)}) %copy-start.3) | copy-done | bytes 65560
  3.4 17.0 %shard_map.46 = f32[128,128]{1,0:T(8,128)S(1)} custom-call(f32[128,128]{1,0:T(8,128)S(1)} %bitcast.6, f32[128,128]{1,0:T(8,128)S(1)} %bitcast.7, f32[128,128]{1,0:T(8,128)S(1)} %bitcast.8, f32[128,128]{1,0:T(8,128)S(1)} %bitcast.9), custom_call_target="tpu_custom_call" | custom-call | tf_op jit(solution)/shard_map/pallas_call | solution.py:242
  20.4 0.6 %copy.6 = f32[8,16,128]{2,1,0:T(8,128)} copy(f32[8,16,128]{2,1,0:T(8,128)S(1)} %bitcast.5) | data formatting | bytes 131072
Async XLA Ops:
  0.0 0.8 %copy-start = (f32[8,16,128]{2,1,0:T(8,128)S(1)}, f32[8,16,128]{2,1,0:T(8,128)}, u32[]{:S(2)}) copy-start(f32[8,16,128]{2,1,0:T(8,128)} %param.4) | copy-start | bytes 196612
  0.8 0.8 %copy-start.1 = (f32[8,16,128]{2,1,0:T(8,128)S(1)}, f32[8,16,128]{2,1,0:T(8,128)}, u32[]{:S(2)}) copy-start(f32[8,16,128]{2,1,0:T(8,128)} %param.5) | copy-start | bytes 196612
  1.7 0.8 %copy-start.2 = (f32[8,16,128]{2,1,0:T(8,128)S(1)}, f32[8,16,128]{2,1,0:T(8,128)}, u32[]{:S(2)}) copy-start(f32[8,16,128]{2,1,0:T(8,128)} %param.6) | copy-start | bytes 196612
  2.5 0.8 %copy-start.3 = (f32[8,16,128]{2,1,0:T(8,128)S(1)}, f32[8,16,128]{2,1,0:T(8,128)}, u32[]{:S(2)}) copy-start(f32[8,16,128]{2,1,0:T(8,128)} %param.7) | copy-start | bytes 196612

commit v2 on v1

--- a/solution.py
+++ b/solution.py
@@ -58,19 +58,32 @@
     return [(pu + t * hu, ps + t * hd) for (pu, ps), (hu, hd) in zip(part, steps)]
 
 
-def kernel(nx, ny, lx, ly, owners, f_ref, kx_ref, ky_ref, r_ref, out_ref,
-           seg_s, seg_r, ent_s, ent_r, yc, yo, sy_v, g_v,
+def kernel(nx, ny, lx, ly, owners, f_hbm, kx_hbm, ky_hbm, r_hbm, out_ref,
+           f_ref, kx_ref, ky_ref, r_ref, load_sems, seg_s, seg_r, ent_s, ent_r, yc, yo, sy_v, g_v,
            seg_ss, seg_rs, ent_ss, ent_rs, yc_ss, yc_rs, yo_ss, yo_rs):
     gx, gy = lax.axis_index("gx"), lax.axis_index("gy")
-    every = nx // owners
     rows = ly // owners
-    mine = gx // every
+    base = (nx - owners) // 2
+    mine = lax.rem(gx + (nx - base), owners)
+    is_owner = (gx >= base) & (gx < base + owners)
+    far_first = sorted(range(1, owners), key=lambda k: abs(k - owners / 2))
+    far_first_x = sorted(range(1, nx), key=lambda k: abs(k - nx / 2))
 
     barrier = pltpu.get_barrier_semaphore()
     for k in range(1, nx):
         pl.semaphore_signal(barrier, inc=1, device_id=(lax.rem(gx + k, nx), gy), device_id_type=MESH)
     for k in range(1, ny):
         pl.semaphore_signal(barrier, inc=1, device_id=(gx, lax.rem(gy + k, ny)), device_id_type=MESH)
+
+    loads = [
+        pltpu.make_async_copy(src, dst, load_sems.at[n])
+        for n, (src, dst) in enumerate(
+            ((kx_hbm, kx_ref), (r_hbm, r_ref), (f_hbm, f_ref), (ky_hbm, ky_ref)))
+    ]
+    for load in loads:
+        load.start()
+    for load in loads[:3]:
+        load.wait()
 
     one = jnp.ones((ly, f_ref.shape[1]), jnp.float32)
     zero = jnp.zeros_like(one)
@@ -92,14 +105,16 @@
         return pltpu.make_async_remote_copy(
             src_ref=seg_s.at[o], dst_ref=seg_r.at[gx],
             send_sem=seg_ss.at[o], recv_sem=seg_rs.at[gx],
-            device_id=(o * every, gy), device_id_type=MESH)
-
-    for k in range(1, owners):
-        seg_copy(lax.rem(mine + k, owners)).start()
-    if every > 1:
-        @pl.when(lax.rem(gx, every) != 0)
+            device_id=(base + o, gy), device_id_type=MESH)
+
+    if owners < nx:
+        @pl.when(jnp.logical_not(is_owner))
         def _():
             seg_copy(mine).start()
+    for k in far_first:
+        seg_copy(lax.rem(mine + k, owners)).start()
+
+    loads[3].wait()
 
     ivals = []
     for i in range(lx):
@@ -155,12 +170,12 @@
         for d, (u, s) in enumerate(join(maps, offs, join_coefs(maps, long), long)):
             ent_s[d, 0] = u
             ent_s[d, 1] = s
-        for k in range(1, nx):
+        for k in far_first_x:
             ent_copy(lax.rem(gx + k, nx)).start()
         ent_r[mine] = ent_s[gx]
 
-    if every > 1:
-        pl.when(lax.rem(gx, every) == 0)(own)
+    if owners < nx:
+        pl.when(is_owner)(own)
     else:
         own()
 
@@ -174,12 +189,12 @@
         pltpu.make_async_remote_copy(
             src_ref=ent_s.at[0], dst_ref=ent_r.at[o],
             send_sem=ent_ss.at[0], recv_sem=ent_rs.at[o],
-            device_id=(o * every, gy), device_id_type=MESH).wait_recv()
+            device_id=(base + o, gy), device_id_type=MESH).wait_recv()
 
     for k in range(1, owners):
         ent_arrived(lax.rem(mine + k, owners))
-    if every > 1:
-        @pl.when(lax.rem(gx, every) != 0)
+    if owners < nx:
+        @pl.when(jnp.logical_not(is_owner))
         def _():
             ent_arrived(mine)
 
@@ -210,8 +225,8 @@
 
     for k in range(1, owners):
         seg_copy(lax.rem(mine + k, owners)).wait_send()
-    if every > 1:
-        @pl.when(lax.rem(gx, every) != 0)
+    if owners < nx:
+        @pl.when(jnp.logical_not(is_owner))
         def _():
             seg_copy(mine).wait_send()
 
@@ -219,8 +234,8 @@
         for k in range(1, nx):
             ent_copy(lax.rem(gx + k, nx)).wait_send()
 
-    if every > 1:
-        pl.when(lax.rem(gx, every) == 0)(own_sent)
+    if owners < nx:
+        pl.when(is_owner)(own_sent)
     else:
         own_sent()
     for k in range(1, ny):
@@ -233,18 +248,22 @@
 
     def per_device(source, coupling_x, coupling_y, reaction):
         lx, ly, nz = source.shape
-        owners = min(nx, ly // 2)
+        owners = min(nx, ly // 4)
         rows = ly // owners
         f32 = jnp.float32
         dma = pltpu.SemaphoreType.DMA
         vmem = pl.BlockSpec(memory_space=pltpu.VMEM)
-        flat = [a.reshape(lx * ly, nz) for a in (source, coupling_x, coupling_y, reaction)]
+        flat = [
+            pltpu.with_memory_space_constraint(a.reshape(lx * ly, nz), pltpu.HBM)
+            for a in (source, coupling_x, coupling_y, reaction)
+        ]
         out = pl.pallas_call(
             functools.partial(kernel, nx, ny, lx, ly, owners),
             out_shape=jax.ShapeDtypeStruct((lx * ly, nz), f32),
-            in_specs=[vmem] * 4,
+            in_specs=[pl.BlockSpec(memory_space=pltpu.HBM)] * 4,
             out_specs=vmem,
             scratch_shapes=[
+                *[pltpu.VMEM((lx * ly, nz), f32)] * 4, dma((4,)),
                 pltpu.VMEM((owners, 6, rows, nz), f32),
                 pltpu.VMEM((nx, 6, rows, nz), f32),
                 pltpu.VMEM((nx, 2, rows, nz), f32),
@@ -257,7 +276,7 @@
                 dma((ny,)), dma((ny,)), dma((ny,)), dma((ny,)),
             ],
             compiler_params=pltpu.CompilerParams(
-                collective_id=0, has_side_effects=True, vmem_limit_bytes=8 * 1024 * 1024),
+                collective_id=0, has_side_effects=True, vmem_limit_bytes=16 * 1024 * 1024),
         )(*flat)
         return out.reshape(lx, ly, nz)
 

time: 21.3 us -> 16.7 us (0.78)
  local copies, waits for them, and re-layouts: 3.99 us -> 0.63 us
  Pallas kernels: 17 us -> 15.9 us
    unnamed x9 -> x1, local copies, waits for them, and re-layouts: 3.99 us -> 0.63 us
    pallas_call x1, Pallas kernels: 17 us -> 15.9 us  [per_device(): pl.pallas_call(functools.partial(kernel, nx, ny, lx, ly, owners), out_sha...]
where the time goes in v2:
time: 16.7 us; the launch traced here: 16.5 us
  Pallas kernels  15.9 us (95%)
  local copies, waits for them, and re-layouts  0.63 us (4%)
    pallas_call x1, Pallas kernels, per_device(): pl.pallas_call(functools.partial(kernel, nx, ny, lx, ly, owners), out_sha...  15.9 us
    unnamed x1, local copies, waits for them, and re-layouts  0.63 us

profile of v2, /device:TPU:0, one launch (start us, length us, event | category | flops | bytes accessed | tf_op | source)
XLA Modules:
  0.0 16.5 jit_solution(9998106365719032691)
XLA Ops:
  0.0 15.9 %shard_map.46 = f32[128,128]{1,0:T(8,128)S(1)} custom-call(f32[128,128]{1,0:T(8,128)} %bitcast.6, f32[128,128]{1,0:T(8,128)} %bitcast.7, f32[128,128]{1,0:T(8,128)} %bitcast.8, f32[128,128]{1,0:T(8,128)} %bitcast.9), custom_call_target="tpu_custom_call" | custom-call | tf_op jit(solution)/shard_map/pallas_call | solution.py:260
  15.9 0.6 %copy.6 = f32[8,16,128]{2,1,0:T(8,128)} copy(f32[8,16,128]{2,1,0:T(8,128)S(1)} %bitcast.5) | data formatting | bytes 131072

commit v3 on v2

--- a/solution.py
+++ b/solution.py
@@ -70,10 +70,11 @@
     far_first_x = sorted(range(1, nx), key=lambda k: abs(k - nx / 2))
 
     barrier = pltpu.get_barrier_semaphore()
-    for k in range(1, nx):
-        pl.semaphore_signal(barrier, inc=1, device_id=(lax.rem(gx + k, nx), gy), device_id_type=MESH)
-    for k in range(1, ny):
-        pl.semaphore_signal(barrier, inc=1, device_id=(gx, lax.rem(gy + k, ny)), device_id_type=MESH)
+
+    @pl.when(is_owner)
+    def _():
+        for k in far_first_x:
+            pl.semaphore_signal(barrier, inc=1, device_id=(lax.rem(gx + k, nx), gy), device_id_type=MESH)
 
     loads = [
         pltpu.make_async_copy(src, dst, load_sems.at[n])
@@ -82,6 +83,8 @@
     ]
     for load in loads:
         load.start()
+    for k in range(1, ny):
+        pl.semaphore_signal(barrier, inc=1, device_id=(gx, lax.rem(gy + k, ny)), device_id_type=MESH)
     for load in loads[:3]:
         load.wait()
 
@@ -95,11 +98,11 @@
         s, g = r_ref[at, :] * inv, f_ref[at, :] * inv
         h1, h2, h3 = sweep(*h1, s, None), sweep(*h2, s, None), sweep(*h3, s, g)
         cells.append((h1[0], h2[0], h3[0]))
-    for v, val in enumerate((h1[0], h2[0], h1[1], h2[1], h3[0], h3[1])):
+    for v, val in enumerate((h1[0], h2[0], h1[1], h3[0], h3[1])):
         for o in range(owners):
             seg_s[o, v] = val[o * rows:(o + 1) * rows, :]
 
-    pl.semaphore_wait(barrier, nx - 1 + ny - 1)
+    pl.semaphore_wait(barrier, owners + ny - 1 - is_owner.astype(jnp.int32))
 
     def seg_copy(o):
         return pltpu.make_async_remote_copy(
@@ -164,8 +167,11 @@
                 src_ref=seg_s.at[0], dst_ref=seg_r.at[frm],
                 send_sem=seg_ss.at[0], recv_sem=seg_rs.at[frm],
                 device_id=(frm, gy), device_id_type=MESH).wait_recv()
-        maps = [tuple(seg_r[d, v] for v in range(4)) for d in range(nx)]
-        offs = [tuple(seg_r[d, v] for v in (4, 5)) for d in range(nx)]
+        maps = []
+        for d in range(nx):
+            a, b, c = (seg_r[d, v] for v in range(3))
+            maps.append((a, b, c, (1.0 + b * c) / a))
+        offs = [(seg_r[d, 3], seg_r[d, 4]) for d in range(nx)]
         long = nx * lx > LONG
         for d, (u, s) in enumerate(join(maps, offs, join_coefs(maps, long), long)):
             ent_s[d, 0] = u
@@ -248,7 +254,7 @@
 
     def per_device(source, coupling_x, coupling_y, reaction):
         lx, ly, nz = source.shape
-        owners = min(nx, ly // 4)
+        owners = min(nx, ly // 8)
         rows = ly // owners
         f32 = jnp.float32
         dma = pltpu.SemaphoreType.DMA
@@ -264,8 +270,8 @@
             out_specs=vmem,
             scratch_shapes=[
                 *[pltpu.VMEM((lx * ly, nz), f32)] * 4, dma((4,)),
-                pltpu.VMEM((owners, 6, rows, nz), f32),
-                pltpu.VMEM((nx, 6, rows, nz), f32),
+                pltpu.VMEM((owners, 5, rows, nz), f32),
+                pltpu.VMEM((nx, 5, rows, nz), f32),
                 pltpu.VMEM((nx, 2, rows, nz), f32),
                 pltpu.VMEM((owners, 2, rows, nz), f32),
                 pltpu.VMEM((ny, 4, lx, nz), f32),

time: 16.7 us -> 15.8 us (0.946)
  Pallas kernels: 15.9 us -> 15 us
    pallas_call x1, Pallas kernels: 15.9 us -> 15 us  [per_device(): pl.pallas_call(functools.partial(kernel, nx, ny, lx, ly, owners), out_sha...]
where the time goes in v3:
time: 15.8 us; the launch traced here: 15.6 us
  Pallas kernels  15 us (95%)
  local copies, waits for them, and re-layouts  0.63 us (4%)
    pallas_call x1, Pallas kernels, per_device(): pl.pallas_call(functools.partial(kernel, nx, ny, lx, ly, owners), out_sha...  15 us
    unnamed x1, local copies, waits for them, and re-layouts  0.63 us

profile of v3, /device:TPU:0, one launch (start us, length us, event | category | flops | bytes accessed | tf_op | source)
XLA Modules:
  0.0 15.6 jit_solution(16705822537196357330)
XLA Ops:
  0.0 15.0 %shard_map.46 = f32[128,128]{1,0:T(8,128)S(1)} custom-call(f32[128,128]{1,0:T(8,128)} %bitcast.6, f32[128,128]{1,0:T(8,128)} %bitcast.7, f32[128,128]{1,0:T(8,128)} %bitcast.8, f32[128,128]{1,0:T(8,128)} %bitcast.9), custom_call_target="tpu_custom_call" | custom-call | tf_op jit(solution)/shard_map/pallas_call | solution.py:266
  15.0 0.6 %copy.6 = f32[8,16,128]{2,1,0:T(8,128)} copy(f32[8,16,128]{2,1,0:T(8,128)S(1)} %bitcast.5) | data formatting | bytes 131072

commit v4 on v3

--- a/solution.py
+++ b/solution.py
@@ -58,22 +58,32 @@
     return [(pu + t * hu, ps + t * hd) for (pu, ps), (hu, hd) in zip(part, steps)]
 
 
+def total(terms):
+    while len(terms) > 1:
+        terms = [sum(terms[k + 1:k + 2], terms[k]) for k in range(0, len(terms), 2)]
+    return terms[0]
+
+
 def kernel(nx, ny, lx, ly, owners, f_hbm, kx_hbm, ky_hbm, r_hbm, out_ref,
-           f_ref, kx_ref, ky_ref, r_ref, load_sems, seg_s, seg_r, ent_s, ent_r, yc, yo, sy_v, g_v,
+           f_ref, kx_ref, ky_ref, r_ref, load_sems, seg_s, seg_r, ent_s, ent_r, yc, yo, sy_v, fa_v, fb_v, fc_v,
            seg_ss, seg_rs, ent_ss, ent_rs, yc_ss, yc_rs, yo_ss, yo_rs):
     gx, gy = lax.axis_index("gx"), lax.axis_index("gy")
     rows = ly // owners
     base = (nx - owners) // 2
     mine = lax.rem(gx + (nx - base), owners)
     is_owner = (gx >= base) & (gx < base + owners)
-    far_first = sorted(range(1, owners), key=lambda k: abs(k - owners / 2))
-    far_first_x = sorted(range(1, nx), key=lambda k: abs(k - nx / 2))
+
+    def elsewhere(d, act):
+        if base <= d < base + owners:
+            pl.when(gx != d)(lambda: act() and None)
+        else:
+            act()
 
     barrier = pltpu.get_barrier_semaphore()
 
     @pl.when(is_owner)
     def _():
-        for k in far_first_x:
+        for k in range(1, nx):
             pl.semaphore_signal(barrier, inc=1, device_id=(lax.rem(gx + k, nx), gy), device_id_type=MESH)
 
     loads = [
@@ -110,12 +120,8 @@
             send_sem=seg_ss.at[o], recv_sem=seg_rs.at[gx],
             device_id=(base + o, gy), device_id_type=MESH)
 
-    if owners < nx:
-        @pl.when(jnp.logical_not(is_owner))
-        def _():
-            seg_copy(mine).start()
-    for k in far_first:
-        seg_copy(lax.rem(mine + k, owners)).start()
+    for o in range(owners):
+        elsewhere(base + o, seg_copy(o).start)
 
     loads[3].wait()
 
@@ -136,22 +142,28 @@
     for v, val in enumerate((y1[0], y2[0], y1[1], y2[1])):
         yc[gy, v] = val
 
-    def y_copy(buf, ss, rs, k):
-        to = lax.rem(gy + k, ny)
+    def y_copy(buf, ss, rs, to):
         return pltpu.make_async_remote_copy(
             src_ref=buf.at[gy], dst_ref=buf.at[gy],
             send_sem=ss.at[to], recv_sem=rs.at[gy],
             device_id=(gx, to), device_id_type=MESH)
 
-    def y_arrived(buf, ss, rs, k):
-        frm = lax.rem(gy + k, ny)
-        pltpu.make_async_remote_copy(
-            src_ref=buf.at[frm], dst_ref=buf.at[frm],
-            send_sem=ss.at[frm], recv_sem=rs.at[frm],
-            device_id=(gx, frm), device_id_type=MESH).wait_recv()
-
-    for k in range(1, ny):
-        y_copy(yc, yc_ss, yc_rs, k).start()
+    def y_all(buf, ss, rs, act):
+        for d in range(ny):
+            @pl.when(gy != d)
+            def _():
+                getattr(y_copy(buf, ss, rs, d), act)()
+
+    def y_arrived(buf, ss, rs):
+        for d in range(ny):
+            @pl.when(gy != d)
+            def _():
+                pltpu.make_async_remote_copy(
+                    src_ref=buf.at[d], dst_ref=buf.at[d],
+                    send_sem=ss.at[d], recv_sem=rs.at[d],
+                    device_id=(gx, d), device_id_type=MESH).wait_recv()
+
+    y_all(yc, yc_ss, yc_rs, "start")
 
     def ent_copy(to):
         return pltpu.make_async_remote_copy(
@@ -161,12 +173,11 @@
 
     def own():
         seg_r[gx] = seg_s[mine]
-        for k in range(1, nx):
-            frm = lax.rem(gx + k, nx)
-            pltpu.make_async_remote_copy(
-                src_ref=seg_s.at[0], dst_ref=seg_r.at[frm],
-                send_sem=seg_ss.at[0], recv_sem=seg_rs.at[frm],
-                device_id=(frm, gy), device_id_type=MESH).wait_recv()
+        for d in range(nx):
+            elsewhere(d, pltpu.make_async_remote_copy(
+                src_ref=seg_s.at[0], dst_ref=seg_r.at[d],
+                send_sem=seg_ss.at[0], recv_sem=seg_rs.at[d],
+                device_id=(d, gy), device_id_type=MESH).wait_recv)
         maps = []
         for d in range(nx):
             a, b, c = (seg_r[d, v] for v in range(3))
@@ -176,8 +187,7 @@
         for d, (u, s) in enumerate(join(maps, offs, join_coefs(maps, long), long)):
             ent_s[d, 0] = u
             ent_s[d, 1] = s
-        for k in far_first_x:
-            ent_copy(lax.rem(gx + k, nx)).start()
+            elsewhere(d, ent_copy(d).start)
         ent_r[mine] = ent_s[gx]
 
     if owners < nx:
@@ -185,41 +195,43 @@
     else:
         own()
 
-    for k in range(1, ny):
-        y_arrived(yc, yc_ss, yc_rs, k)
+    y_arrived(yc, yc_ss, yc_rs)
     ymaps = [tuple(yc[d, v] for v in range(4)) for d in range(ny)]
     ylong = ny * ly > LONG
     ycoefs = join_coefs(ymaps, ylong)
 
-    def ent_arrived(o):
-        pltpu.make_async_remote_copy(
+    for i, val in enumerate(cells):
+        for buf, part in zip((fa_v, fb_v, fc_v), val):
+            buf[pl.ds(i * ly, ly), :] = part * ivals[i]
+    turned = [
+        tuple(buf[pl.ds(j, lx, stride=ly), :] for buf in (fa_v, fb_v, fc_v)) for j in range(ly)
+    ]
+    up, us, qp, qs, weights = one8, zero8, zero8, one8, []
+    for j in reversed(range(ly)):
+        weights.append((us, qs))
+        up, qp = up + sy[j] * us, qp + sy[j] * qs
+        us, qs = us + up, qs + qp
+    weights = weights[::-1]
+
+    for o in range(owners):
+        elsewhere(base + o, pltpu.make_async_remote_copy(
             src_ref=ent_s.at[0], dst_ref=ent_r.at[o],
             send_sem=ent_ss.at[0], recv_sem=ent_rs.at[o],
-            device_id=(base + o, gy), device_id_type=MESH).wait_recv()
-
-    for k in range(1, owners):
-        ent_arrived(lax.rem(mine + k, owners))
-    if owners < nx:
-        @pl.when(jnp.logical_not(is_owner))
-        def _():
-            ent_arrived(mine)
-
-    u0 = jnp.concatenate([ent_r[o, 0] for o in range(owners)], axis=0)
-    s0 = jnp.concatenate([ent_r[o, 1] for o in range(owners)], axis=0)
-    for i in range(lx):
-        ca, cb, cg = cells[i]
-        g_v[pl.ds(i * ly, ly), :] = ((ca * u0 + cb * s0) + cg) * ivals[i]
-
+            device_id=(base + o, gy), device_id_type=MESH).wait_recv)
+
+    g_y = []
+    for j in range(ly):
+        o, row = j // rows, pl.ds(j % rows, 1)
+        fa, fb, fc = turned[j]
+        g_y.append((fa * ent_r[o, 0, row, :] + fb * ent_r[o, 1, row, :]) + fc)
+    yo[gy, 0] = -total([w[0] * g for w, g in zip(weights, g_y)])
+    yo[gy, 1] = -total([w[1] * g for w, g in zip(weights, g_y)])
+    y_all(yo, yo_ss, yo_rs, "start")
     y3, ygs = (zero8, zero8), []
     for j in range(ly):
-        y3 = sweep(*y3, sy[j], g_v[pl.ds(j, lx, stride=ly), :])
+        y3 = sweep(*y3, sy[j], g_y[j])
         ygs.append(y3[0])
-    yo[gy, 0] = y3[0]
-    yo[gy, 1] = y3[1]
-    for k in range(1, ny):
-        y_copy(yo, yo_ss, yo_rs, k).start()
-    for k in range(1, ny):
-        y_arrived(yo, yo_ss, yo_rs, k)
+    y_arrived(yo, yo_ss, yo_rs)
     yoffs = [(yo[d, 0], yo[d, 1]) for d in range(ny)]
     u, s = zero8, zero8
     for d, (du, ds) in enumerate(join(ymaps, yoffs, ycoefs, ylong)):
@@ -229,24 +241,19 @@
         ca, cb = ycells[j]
         out_ref[pl.ds(j, lx, stride=ly), :] = (ca * u + cb * s) + ygs[j]
 
-    for k in range(1, owners):
-        seg_copy(lax.rem(mine + k, owners)).wait_send()
-    if owners < nx:
-        @pl.when(jnp.logical_not(is_owner))
-        def _():
-            seg_copy(mine).wait_send()
+    for o in range(owners):
+        elsewhere(base + o, seg_copy(o).wait_send)
 
     def own_sent():
-        for k in range(1, nx):
-            ent_copy(lax.rem(gx + k, nx)).wait_send()
+        for d in range(nx):
+            elsewhere(d, ent_copy(d).wait_send)
 
     if owners < nx:
         pl.when(is_owner)(own_sent)
     else:
         own_sent()
-    for k in range(1, ny):
-        y_copy(yc, yc_ss, yc_rs, k).wait_send()
-        y_copy(yo, yo_ss, yo_rs, k).wait_send()
+    y_all(yc, yc_ss, yc_rs, "wait_send")
+    y_all(yo, yo_ss, yo_rs, "wait_send")
 
 
 def solution(mesh):
@@ -276,8 +283,7 @@
                 pltpu.VMEM((owners, 2, rows, nz), f32),
                 pltpu.VMEM((ny, 4, lx, nz), f32),
                 pltpu.VMEM((ny, 2, lx, nz), f32),
-                pltpu.VMEM((lx * ly, nz), f32),
-                pltpu.VMEM((lx * ly, nz), f32),
+                *[pltpu.VMEM((lx * ly, nz), f32)] * 4,
                 dma((owners,)), dma((nx,)), dma((nx,)), dma((owners,)),
                 dma((ny,)), dma((ny,)), dma((ny,)), dma((ny,)),
             ],

time: 15.8 us -> 15.9 us (level)
  no operation moved by 1% of the time
where the time goes in v4:
time: 15.9 us; the launch traced here: 15.8 us
  Pallas kernels  15.1 us (95%)
  local copies, waits for them, and re-layouts  0.63 us (4%)
    pallas_call x1, Pallas kernels, per_device(): pl.pallas_call(functools.partial(kernel, nx, ny, lx, ly, owners), out_sha...  15.1 us
    unnamed x1, local copies, waits for them, and re-layouts  0.63 us

profile of v4, /device:TPU:0, one launch (start us, length us, event | category | flops | bytes accessed | tf_op | source)
XLA Modules:
  0.0 15.8 jit_solution(12319324898512904709)
XLA Ops:
  0.0 15.1 %shard_map.46 = f32[128,128]{1,0:T(8,128)S(1)} custom-call(f32[128,128]{1,0:T(8,128)} %bitcast.6, f32[128,128]{1,0:T(8,128)} %bitcast.7, f32[128,128]{1,0:T(8,128)} %bitcast.8, f32[128,128]{1,0:T(8,128)} %bitcast.9), custom_call_target="tpu_custom_call" | custom-call | tf_op jit(solution)/shard_map/pallas_call | solution.py:273
  15.1 0.6 %copy.6 = f32[8,16,128]{2,1,0:T(8,128)} copy(f32[8,16,128]{2,1,0:T(8,128)S(1)} %bitcast.5) | data formatting | bytes 131072

commit v5 on v4

--- a/solution.py
+++ b/solution.py
@@ -64,13 +64,16 @@
     return terms[0]
 
 
-def kernel(nx, ny, lx, ly, owners, f_hbm, kx_hbm, ky_hbm, r_hbm, out_ref,
+def kernel(nx, ny, lx, ly, groups, f_hbm, kx_hbm, ky_hbm, r_hbm, out_ref,
            f_ref, kx_ref, ky_ref, r_ref, load_sems, seg_s, seg_r, ent_s, ent_r, yc, yo, sy_v, fa_v, fb_v, fc_v,
            seg_ss, seg_rs, ent_ss, ent_rs, yc_ss, yc_rs, yo_ss, yo_rs):
     gx, gy = lax.axis_index("gx"), lax.axis_index("gy")
-    rows = ly // owners
-    base = (nx - owners) // 2
-    mine = lax.rem(gx + (nx - base), owners)
+    rows, half, owners = ly // groups, nx // 2, 2 * groups
+    base = half - groups
+    upper = (gx >= half).astype(jnp.int32)
+    first = upper * half
+    server = base + upper * groups
+    mine = lax.rem(gx + (nx * groups - base), groups)
     is_owner = (gx >= base) & (gx < base + owners)
 
     def elsewhere(d, act):
@@ -109,14 +112,14 @@
         h1, h2, h3 = sweep(*h1, s, None), sweep(*h2, s, None), sweep(*h3, s, g)
         cells.append((h1[0], h2[0], h3[0]))
     for v, val in enumerate((h1[0], h2[0], h1[1], h3[0], h3[1])):
-        for o in range(owners):
+        for o in range(groups):
             seg_s[o, v] = val[o * rows:(o + 1) * rows, :]
 
     pl.semaphore_wait(barrier, owners + ny - 1 - is_owner.astype(jnp.int32))
 
     def seg_copy(o):
         return pltpu.make_async_remote_copy(
-            src_ref=seg_s.at[o], dst_ref=seg_r.at[gx],
+            src_ref=seg_s.at[o % groups], dst_ref=seg_r.at[gx],
             send_sem=seg_ss.at[o], recv_sem=seg_rs.at[gx],
             device_id=(base + o, gy), device_id_type=MESH)
 
@@ -187,7 +190,10 @@
         for d, (u, s) in enumerate(join(maps, offs, join_coefs(maps, long), long)):
             ent_s[d, 0] = u
             ent_s[d, 1] = s
-            elsewhere(d, ent_copy(d).start)
+        for k in range(half):
+            @pl.when(gx != first + k)
+            def _():
+                ent_copy(first + k).start()
         ent_r[mine] = ent_s[gx]
 
     if owners < nx:
@@ -213,11 +219,13 @@
         us, qs = us + up, qs + qp
     weights = weights[::-1]
 
-    for o in range(owners):
-        elsewhere(base + o, pltpu.make_async_remote_copy(
-            src_ref=ent_s.at[0], dst_ref=ent_r.at[o],
-            send_sem=ent_ss.at[0], recv_sem=ent_rs.at[o],
-            device_id=(base + o, gy), device_id_type=MESH).wait_recv)
+    for o in range(groups):
+        @pl.when(gx != server + o)
+        def _():
+            pltpu.make_async_remote_copy(
+                src_ref=ent_s.at[0], dst_ref=ent_r.at[o],
+                send_sem=ent_ss.at[0], recv_sem=ent_rs.at[o],
+                device_id=(server + o, gy), device_id_type=MESH).wait_recv()
 
     g_y = []
     for j in range(ly):
@@ -231,6 +239,23 @@
     for j in range(ly):
         y3 = sweep(*y3, sy[j], g_y[j])
         ygs.append(y3[0])
+
+    for o in range(owners):
+        elsewhere(base + o, seg_copy(o).wait_send)
+
+    def own_sent():
+        for k in range(half):
+            @pl.when(gx != first + k)
+            def _():
+                ent_copy(first + k).wait_send()
+
+    if owners < nx:
+        pl.when(is_owner)(own_sent)
+    else:
+        own_sent()
+    y_all(yc, yc_ss, yc_rs, "wait_send")
+    y_all(yo, yo_ss, yo_rs, "wait_send")
+
     y_arrived(yo, yo_ss, yo_rs)
     yoffs = [(yo[d, 0], yo[d, 1]) for d in range(ny)]
     u, s = zero8, zero8
@@ -241,28 +266,14 @@
         ca, cb = ycells[j]
         out_ref[pl.ds(j, lx, stride=ly), :] = (ca * u + cb * s) + ygs[j]
 
-    for o in range(owners):
-        elsewhere(base + o, seg_copy(o).wait_send)
-
-    def own_sent():
-        for d in range(nx):
-            elsewhere(d, ent_copy(d).wait_send)
-
-    if owners < nx:
-        pl.when(is_owner)(own_sent)
-    else:
-        own_sent()
-    y_all(yc, yc_ss, yc_rs, "wait_send")
-    y_all(yo, yo_ss, yo_rs, "wait_send")
-
 
 def solution(mesh):
     nx, ny = mesh.shape["gx"], mesh.shape["gy"]
 
     def per_device(source, coupling_x, coupling_y, reaction):
         lx, ly, nz = source.shape
-        owners = min(nx, ly // 8)
-        rows = ly // owners
+        groups = min(nx // 2, ly // 8)
+        owners, rows = 2 * groups, ly // groups
         f32 = jnp.float32
         dma = pltpu.SemaphoreType.DMA
         vmem = pl.BlockSpec(memory_space=pltpu.VMEM)
@@ -271,20 +282,20 @@
             for a in (source, coupling_x, coupling_y, reaction)
         ]
         out = pl.pallas_call(
-            functools.partial(kernel, nx, ny, lx, ly, owners),
+            functools.partial(kernel, nx, ny, lx, ly, groups),
             out_shape=jax.ShapeDtypeStruct((lx * ly, nz), f32),
             in_specs=[pl.BlockSpec(memory_space=pltpu.HBM)] * 4,
             out_specs=vmem,
             scratch_shapes=[
                 *[pltpu.VMEM((lx * ly, nz), f32)] * 4, dma((4,)),
-                pltpu.VMEM((owners, 5, rows, nz), f32),
+                pltpu.VMEM((groups, 5, rows, nz), f32),
                 pltpu.VMEM((nx, 5, rows, nz), f32),
                 pltpu.VMEM((nx, 2, rows, nz), f32),
-                pltpu.VMEM((owners, 2, rows, nz), f32),
+                pltpu.VMEM((groups, 2, rows, nz), f32),
                 pltpu.VMEM((ny, 4, lx, nz), f32),
                 pltpu.VMEM((ny, 2, lx, nz), f32),
                 *[pltpu.VMEM((lx * ly, nz), f32)] * 4,
-                dma((owners,)), dma((nx,)), dma((nx,)), dma((owners,)),
+                dma((owners,)), dma((nx,)), dma((nx,)), dma((groups,)),
                 dma((ny,)), dma((ny,)), dma((ny,)), dma((ny,)),
             ],
             compiler_params=pltpu.CompilerParams(

time: 15.9 us -> 15.3 us (0.962)
  Pallas kernels: 15.1 us -> 14.5 us
    pallas_call x1, Pallas kernels: 15.1 us -> 14.5 us  [per_device(): pl.pallas_call(functools.partial(kernel, nx, ny, lx, ly, groups), out_sha...]
where the time goes in v5:
time: 15.3 us; the launch traced here: 15.1 us
  Pallas kernels  14.5 us (95%)
  local copies, waits for them, and re-layouts  0.63 us (4%)
    pallas_call x1, Pallas kernels, per_device(): pl.pallas_call(functools.partial(kernel, nx, ny, lx, ly, groups), out_sha...  14.5 us
    unnamed x1, local copies, waits for them, and re-layouts  0.63 us

profile of v5, /device:TPU:0, one launch (start us, length us, event | category | flops | bytes accessed | tf_op | source)
XLA Modules:
  0.0 15.1 jit_solution(12662868675354641268)
XLA Ops:
  0.0 14.5 %shard_map.46 = f32[128,128]{1,0:T(8,128)S(1)} custom-call(f32[128,128]{1,0:T(8,128)} %bitcast.6, f32[128,128]{1,0:T(8,128)} %bitcast.7, f32[128,128]{1,0:T(8,128)} %bitcast.8, f32[128,128]{1,0:T(8,128)} %bitcast.9), custom_call_target="tpu_custom_call" | custom-call | tf_op jit(solution)/shard_map/pallas_call | solution.py:284
  14.5 0.6 %copy.6 = f32[8,16,128]{2,1,0:T(8,128)} copy(f32[8,16,128]{2,1,0:T(8,128)S(1)} %bitcast.5) | data formatting | bytes 131072

commit v6 on v5

--- a/solution.py
+++ b/solution.py
@@ -84,11 +84,6 @@
 
     barrier = pltpu.get_barrier_semaphore()
 
-    @pl.when(is_owner)
-    def _():
-        for k in range(1, nx):
-            pl.semaphore_signal(barrier, inc=1, device_id=(lax.rem(gx + k, nx), gy), device_id_type=MESH)
-
     loads = [
         pltpu.make_async_copy(src, dst, load_sems.at[n])
         for n, (src, dst) in enumerate(
@@ -96,6 +91,12 @@
     ]
     for load in loads:
         load.start()
+
+    @pl.when(is_owner)
+    def _():
+        for k in range(1, nx):
+            pl.semaphore_signal(barrier, inc=1, device_id=(lax.rem(gx + k, nx), gy), device_id_type=MESH)
+
     for k in range(1, ny):
         pl.semaphore_signal(barrier, inc=1, device_id=(gx, lax.rem(gy + k, ny)), device_id_type=MESH)
     for load in loads[:3]:
@@ -272,7 +273,7 @@
 
     def per_device(source, coupling_x, coupling_y, reaction):
         lx, ly, nz = source.shape
-        groups = min(nx // 2, ly // 8)
+        groups = max(1, min(nx // 2, ly // 16))
         owners, rows = 2 * groups, ly // groups
         f32 = jnp.float32
         dma = pltpu.SemaphoreType.DMA

time: 15.3 us -> 14.7 us (0.961)
  Pallas kernels: 14.5 us -> 13.9 us
    pallas_call x1, Pallas kernels: 14.5 us -> 13.9 us  [per_device(): pl.pallas_call(functools.partial(kernel, nx, ny, lx, ly, groups), out_sha...]
where the time goes in v6:
time: 14.7 us; the launch traced here: 14.6 us
  Pallas kernels  13.9 us (95%)
  local copies, waits for them, and re-layouts  0.63 us (4%)
    pallas_call x1, Pallas kernels, per_device(): pl.pallas_call(functools.partial(kernel, nx, ny, lx, ly, groups), out_sha...  13.9 us
    unnamed x1, local copies, waits for them, and re-layouts  0.63 us

profile of v6, /device:TPU:0, one launch (start us, length us, event | category | flops | bytes accessed | tf_op | source)
XLA Modules:
  0.0 14.6 jit_solution(16340880779201325448)
XLA Ops:
  0.0 13.9 %shard_map.46 = f32[128,128]{1,0:T(8,128)S(1)} custom-call(f32[128,128]{1,0:T(8,128)} %bitcast.6, f32[128,128]{1,0:T(8,128)} %bitcast.7, f32[128,128]{1,0:T(8,128)} %bitcast.8, f32[128,128]{1,0:T(8,128)} %bitcast.9), custom_call_target="tpu_custom_call" | custom-call | tf_op jit(solution)/shard_map/pallas_call | solution.py:285
  13.9 0.6 %copy.6 = f32[8,16,128]{2,1,0:T(8,128)} copy(f32[8,16,128]{2,1,0:T(8,128)S(1)} %bitcast.5) | data formatting | bytes 131072

commit v7 on v6

--- a/solution.py
+++ b/solution.py
@@ -143,7 +143,7 @@
         sy.append(s)
         y1, y2 = sweep(*y1, s, None), sweep(*y2, s, None)
         ycells.append((y1[0], y2[0]))
-    for v, val in enumerate((y1[0], y2[0], y1[1], y2[1])):
+    for v, val in enumerate((y1[0], y2[0], y1[1])):
         yc[gy, v] = val
 
     def y_copy(buf, ss, rs, to):
@@ -203,7 +203,10 @@
         own()
 
     y_arrived(yc, yc_ss, yc_rs)
-    ymaps = [tuple(yc[d, v] for v in range(4)) for d in range(ny)]
+    ymaps = []
+    for d in range(ny):
+        a, b, c = (yc[d, v] for v in range(3))
+        ymaps.append((a, b, c, (1.0 + b * c) / a))
     ylong = ny * ly > LONG
     ycoefs = join_coefs(ymaps, ylong)
 
@@ -293,7 +296,7 @@
                 pltpu.VMEM((nx, 5, rows, nz), f32),
                 pltpu.VMEM((nx, 2, rows, nz), f32),
                 pltpu.VMEM((groups, 2, rows, nz), f32),
-                pltpu.VMEM((ny, 4, lx, nz), f32),
+                pltpu.VMEM((ny, 3, lx, nz), f32),
                 pltpu.VMEM((ny, 2, lx, nz), f32),
                 *[pltpu.VMEM((lx * ly, nz), f32)] * 4,
                 dma((owners,)), dma((nx,)), dma((nx,)), dma((groups,)),

time: 14.7 us -> 14.7 us (level)
  no operation moved by 1% of the time
where the time goes in v7:
time: 14.7 us; the launch traced here: 14.6 us
  Pallas kernels  13.9 us (95%)
  local copies, waits for them, and re-layouts  0.63 us (4%)
    pallas_call x1, Pallas kernels, per_device(): pl.pallas_call(functools.partial(kernel, nx, ny, lx, ly, groups), out_sha...  13.9 us
    unnamed x1, local copies, waits for them, and re-layouts  0.63 us

profile of v7, /device:TPU:0, one launch (start us, length us, event | category | flops | bytes accessed | tf_op | source)
XLA Modules:
  0.0 14.6 jit_solution(6540667949779615513)
XLA Ops:
  0.0 13.9 %shard_map.46 = f32[128,128]{1,0:T(8,128)S(1)} custom-call(f32[128,128]{1,0:T(8,128)} %bitcast.6, f32[128,128]{1,0:T(8,128)} %bitcast.7, f32[128,128]{1,0:T(8,128)} %bitcast.8, f32[128,128]{1,0:T(8,128)} %bitcast.9), custom_call_target="tpu_custom_call" | custom-call | tf_op jit(solution)/shard_map/pallas_call | solution.py:288
  13.9 0.6 %copy.6 = f32[8,16,128]{2,1,0:T(8,128)} copy(f32[8,16,128]{2,1,0:T(8,128)S(1)} %bitcast.5) | data formatting | bytes 131072
